TPU v7x, 256 devices: a whole 4x4x8 slice. The times are simulated.
256 devices in a mesh: dp: 4 (over y), ctx: 64 (over x, z, core).
Axes of the slice: x: 4, y: 4, z: 8, core: 2. Of those that a mesh axis runs over, the one named last changes fastest.
Arguments:
- query_rows: bfloat16 [163840, 1152], P(('dp', 'ctx')), parts along dimension 0, may hold values from -6 to 6
- key_rows: bfloat16 [163840, 1152], P(('dp', 'ctx')), parts along dimension 0, may hold values from -6 to 6
- value_rows: bfloat16 [163840, 1152], P(('dp', 'ctx')), parts along dimension 0, may hold values from -6 to 6
- out_grad: bfloat16 [163840, 1152], P(('dp', 'ctx')), parts along dimension 0, may hold values from -24 to 24
- logsumexp: bfloat16 [163840, 16], P(('dp', 'ctx')), parts along dimension 0, may hold values from 5 to 7
- row_delta: bfloat16 [163840, 16], P(('dp', 'ctx')), parts along dimension 0, may hold values from -48 to 48
- local_members: int32 [512, 256], P(('dp', 'ctx')), parts along dimension 0, may hold values from 0 to 639, as said below
- send_rows: int32 [256, 64, 8], P(('dp', 'ctx')), parts along dimension 0, may hold values from 0 to 640, as said below
- window_slots: int32 [256, 256], P(('dp', 'ctx')), parts along dimension 0, may hold values from 0 to 511, as said below
- window_owner: int32 [256], P('dp'), parts along dimension 0, may hold values from 0 to 63, as said below
Outputs:
- grad_query: bfloat16 [163840, 1152], P(('dp', 'ctx')), parts along dimension 0
- grad_key: bfloat16 [163840, 1152], P(('dp', 'ctx')), parts along dimension 0
- grad_value: bfloat16 [163840, 1152], P(('dp', 'ctx')), parts along dimension 0
There are 4 independent parts, one for each index of `dp`. A program takes and returns all parts, laid end to end along the dimension named above; each array names one. Nothing has to cross between parts.
Inputs may be any that keep to these rules, and one draw needn't show every extreme that they name: Row s * 2 + w lists rows of device s; the rows in local_members for device s and the filled entries of send_rows[s] together name each row of device s below 640 exactly once. send_rows[s, o, c] is a row of device s, or 640 for an empty slot; filled slots come first; only devices that own a crossing window get filled slots; each device fills 256 // 2 slots in all; in every draw some device fills all 8 slots to some owner. `window_slots`: the two devices of a pair have equal rows; the row of pair i names each filled slot arriving at the pair's owner exactly once, as s * 8 + c for sender s and slot c. `window_owner`: A permutation of the devices.
All inputs are finite; a program needn't handle non-finite values.
Results may differ from a plain program's by a relative error of at most 0.0054.
Values may be sent and summed in bfloat16 or wider, within the bound.
No kernel may reach another device: no remote copies, remote signals or barrier semaphores. Data moves between devices by JAX's collectives and lax.ppermute only.
A program may use at most 128 MiB of HBM per device.

v0:
```python
import functools

import jax
import jax.numpy as jnp
from jax import lax
from jax.experimental import pallas as pl
from jax.experimental.pallas import tpu as pltpu
from jax.sharding import PartitionSpec as P

LANES = 128
PARAMS = pltpu.CompilerParams(vmem_limit_bytes=50 * 2**20)
NT = (((1,), (1,)), ((), ()))
TN = (((0,), (0,)), ((), ()))


def up(number):
    return -(-number // LANES) * LANES


def dot(left, right, dims=(((1,), (0,)), ((), ()))):
    return lax.dot_general(left, right, dims, preferred_element_type=jnp.float32)


def head_part(pair, head, size, masked):
    ref, base = pair
    first, last = base + head * size, base + (head + 1) * size
    low, high = first // LANES * LANES, up(last)
    part = ref[:, low:high]
    if masked:
        lane = lax.broadcasted_iota(jnp.int32, (1, high - low), 1) + low
        part = jnp.where((lane >= first) & (lane < last), part, jnp.zeros_like(part))
    return part, low, high


def attend(heads, size, query, key, value, grad, lse_of, delta_of, dquery, dkey, dvalue):
    scaling = size ** (-0.5)
    for head in range(heads):
        q_part, _, _ = head_part(query, head, size, True)
        k_part, _, _ = head_part(key, head, size, True)
        v_part, _, _ = head_part(value, head, size, False)
        g_part, _, _ = head_part(grad, head, size, True)
        scores = dot(k_part, q_part, NT) * scaling
        probs = jnp.exp(scores - lse_of(head))
        dprobs = dot(v_part, g_part, NT)
        dscores = (probs * (dprobs - delta_of(head))).astype(jnp.bfloat16)
        for (ref, base), part in (
            (dvalue, dot(probs.astype(jnp.bfloat16), g_part)),
            (dkey, dot(dscores, q_part) * scaling),
            (dquery, dot(dscores, k_part, TN) * scaling),
        ):
            low = (base + head * size) // LANES * LANES
            ref[:, low : low + part.shape[1]] += part


def local_kernel(heads, size, members_ref, q_ref, k_ref, v_ref, g_ref, stats_ref, dq_ref, dk_ref, dv_ref, *scratch):
    gathered, sums, stat_rows = scratch[:4], scratch[4:7], scratch[7]
    tokens, win = q_ref.shape[0], members_ref.shape[0]
    windows = members_ref.shape[1]
    token = lax.broadcasted_iota(jnp.int32, (win, tokens), 1)
    for window in range(windows):
        picker = (members_ref[:, window : window + 1] == token).astype(jnp.bfloat16)
        for source, target in zip((q_ref, k_ref, v_ref, g_ref), gathered):
            target[...] = dot(picker, source[...]).astype(jnp.bfloat16)
        stat_rows[...] = dot(stats_ref[...], picker, NT)
        for total in sums:
            total[...] = jnp.zeros_like(total)
        attend(
            heads,
            size,
            *((ref, 0) for ref in gathered),
            lambda head: stat_rows[head : head + 1, :],
            lambda head: stat_rows[heads + head : heads + head + 1, :],
            *((ref, 0) for ref in sums),
        )
        for total, out in zip(sums, (dq_ref, dk_ref, dv_ref)):
            placed = dot(picker, total[...].astype(jnp.bfloat16), TN).astype(jnp.bfloat16)
            if window == 0:
                out[...] = placed
            else:
                out[...] += placed


def pack_kernel(rows_ref, halves_ref, q_ref, v_ref, k_ref, g_ref, stats_ref, out_ref):
    tokens, width = q_ref.shape
    half = width // 2
    slots = out_ref.shape[0]
    token = lax.broadcasted_iota(jnp.int32, (slots, tokens), 1)
    named = rows_ref[...] == token
    second = halves_ref[...] == 1
    picks = [(named & ~second).astype(jnp.bfloat16), (named & second).astype(jnp.bfloat16)]
    pieces = []
    for ref in (q_ref, v_ref, k_ref, g_ref):
        source = ref[...]
        pieces.append((dot(picks[0], source[:, :half]) + dot(picks[1], source[:, half:])).astype(jnp.bfloat16))
    stats = stats_ref[...]
    kept = stats.shape[1] // 2
    pieces.append((dot(picks[0], stats[:, :kept]) + dot(picks[1], stats[:, kept:])).astype(jnp.bfloat16))
    pieces.append(jnp.zeros((slots, out_ref.shape[1] - 4 * half - kept), jnp.bfloat16))
    out_ref[...] = jnp.concatenate(pieces, 1)


def cross_kernel(heads, size, half, slots_ref, arrived_ref, out_ref, rows, sums, stat_rows):
    win, count = slots_ref.shape[0], arrived_ref.shape[0]
    picker = (slots_ref[...] == lax.broadcasted_iota(jnp.int32, (win, count), 1)).astype(jnp.bfloat16)
    picked = dot(picker, arrived_ref[...])
    rows[...] = picked.astype(jnp.bfloat16)
    stat_rows[...] = picked[:, 4 * half :].T
    sums[...] = jnp.zeros_like(sums)
    attend(
        heads,
        size,
        (rows, 0),
        (rows, 2 * half),
        (rows, half),
        (rows, 3 * half),
        lambda head: stat_rows[head : head + 1, :],
        lambda head: stat_rows[heads + head : heads + head + 1, :],
        (sums, 0),
        (sums, 2 * half),
        (sums, half),
    )
    out_ref[...] = dot(picker, sums[...].astype(jnp.bfloat16), TN).astype(jnp.bfloat16)


def combine_kernel(half, rows_ref, halves_ref, back_ref, lq_ref, lk_ref, lv_ref, dq_ref, dk_ref, dv_ref):
    tokens, slots = lq_ref.shape[0], back_ref.shape[0]
    named = rows_ref[...] == lax.broadcasted_iota(jnp.int32, (tokens, slots), 0)
    second = halves_ref[...] == 1
    placers = [(named & ~second).astype(jnp.bfloat16), (named & second).astype(jnp.bfloat16)]
    back = back_ref[...]
    parts = [dot(placer, back).astype(jnp.bfloat16) for placer in placers]
    for at, (local, out) in enumerate(((lq_ref, dq_ref), (lv_ref, dv_ref), (lk_ref, dk_ref))):
        both = [part[:, at * half : (at + 1) * half] for part in parts]
        out[...] = local[...] + jnp.concatenate(both, 1)


def per_device(
    query_rows,
    key_rows,
    value_rows,
    out_grad,
    logsumexp,
    row_delta,
    local_members,
    send_rows,
    window_slots,
    window_owner,
):
    tokens, width = query_rows.shape
    heads = logsumexp.shape[1]
    size = width // heads
    half = width // 2
    devices, slot_cap = send_rows.shape[1:]
    win = window_slots.shape[1]
    slots = devices * slot_cap
    bf16, f32 = jnp.bfloat16, jnp.float32

    peers = jnp.arange(devices, dtype=jnp.int32)
    named = window_owner[None, :] == peers[:, None]
    first_of_pair = jnp.repeat(window_owner[::2], 2)
    pair_owner = jnp.sum(jnp.where(named, first_of_pair[None, :], 0), 1)
    half_ids = jnp.sum(jnp.where(named, (peers % 2)[None, :], 0), 1)
    half_rows = jnp.sum(jnp.where((pair_owner[:, None] == peers[None, :])[:, :, None], send_rows[0][None], 0), 1)
    half_ids = jnp.broadcast_to(half_ids[:, None], (devices, slot_cap))
    row_col, half_col = half_rows.reshape(slots, 1), half_ids.reshape(slots, 1)
    row_row, half_row = half_rows.reshape(1, slots), half_ids.reshape(1, slots)

    kept = heads // 2
    stat_cols = jnp.concatenate(
        [logsumexp[:, :kept], row_delta[:, :kept], logsumexp[:, kept:], row_delta[:, kept:]], 1
    )
    sent_width = up(4 * half + heads)
    outgoing = pl.pallas_call(
        pack_kernel,
        out_shape=jax.ShapeDtypeStruct((slots, sent_width), bf16),
        compiler_params=PARAMS,
    )(row_col, half_col, query_rows, value_rows, key_rows, out_grad, stat_cols)
    arrived = lax.all_to_all(
        outgoing.reshape(devices, slot_cap, sent_width), "ctx", split_axis=0, concat_axis=0, tiled=True
    ).reshape(slots, sent_width)

    stat_lines = jnp.concatenate([logsumexp, row_delta], 1).T
    whole = jax.ShapeDtypeStruct((tokens, width), bf16)
    local = pl.pallas_call(
        functools.partial(local_kernel, heads, size),
        out_shape=(whole,) * 3,
        scratch_shapes=[pltpu.VMEM((win, width), bf16)] * 4
        + [pltpu.VMEM((win, width), f32)] * 3
        + [pltpu.VMEM((2 * heads, win), f32)],
        compiler_params=PARAMS,
    )(local_members.T, query_rows, key_rows, value_rows, out_grad, stat_lines)

    back_width = up(3 * half)
    replies = pl.pallas_call(
        functools.partial(cross_kernel, kept, size, half),
        out_shape=jax.ShapeDtypeStruct((slots, back_width), bf16),
        scratch_shapes=[
            pltpu.VMEM((win, sent_width), bf16),
            pltpu.VMEM((win, back_width), f32),
            pltpu.VMEM((sent_width - 4 * half, win), f32),
        ],
        compiler_params=PARAMS,
    )(window_slots.reshape(win, 1), arrived)
    returned = lax.all_to_all(
        replies.reshape(devices, slot_cap, back_width), "ctx", split_axis=0, concat_axis=0, tiled=True
    ).reshape(slots, back_width)

    return pl.pallas_call(
        functools.partial(combine_kernel, half),
        out_shape=(whole,) * 3,
        compiler_params=PARAMS,
    )(row_row, half_row, returned, *local)


def solution(mesh):
    split = P(("dp", "ctx"), None)
    placed = (split,) * 7 + (P(("dp", "ctx"), None, None), split, P("dp"))
    return jax.shard_map(
        per_device,
        mesh=mesh,
        in_specs=placed,
        out_specs=(split,) * 3,
        check_vma=False,
    )
```

profile of v0, /device:TPU:1, one launch (start us, length us, event | category | flops | bytes accessed | tf_op | source)
XLA Modules:
  0.0 155.8 jit_solution(3797791262368314871)
XLA Ops:
  0.6 0.8 slice.15
  1.5 0.1 broadcast_in_dim.58
  1.6 0.8 select_reduce_fusion.1
  2.4 0.1 iota_compare_fusion
  2.5 0.8 fusion
  3.2 0.2 copy.36.stats_ref
  3.5 0.1 reshape.76.halves_ref
  3.6 1.8 %select_reduce_fusion = s32[64,8]{1,0:T(8,128)S(1)} fusion(s32[64,8]{0,1:T(8,128)} %bitcast.12, pred[64,64]{1,0:T(8,128)(4,1)S(1)} %iota_compare_fusion), kind=kLoop, calls=%fused_computation | loop fusion | flops 65024 | bytes 8192 | tf_op jit(solution)/shard_map/reduce_sum | solution.py:163
  5.5 0.1 reshape.75.rows_ref
  5.6 1.4 copy-done
  7.0 1.4 copy-done.1
  8.3 8.7 %shard_map.121 = bf16[512,2432]{1,0:T(8,128)(2,1)} custom-call(s32[512,1]{1,0:T(8,128)S(1)} %reshape.75.rows_ref, s32[512,1]{1,0:T(8,128)S(1)} %reshape.76.halves_ref, bf16[640,1152]{1,0:T(8,128)(2,1)S(1)} %copy-done, bf16[640,1152]{1,0:T(8,128)(2,1)S(1)} %copy-done.1, bf16[640,1152]{1,0:T(8,128)(2,1)} %k_ref.3, bf16[640,1152]{1,0:T(8,128)(2,1)} %g_ref.3, ...), custom_call_target="tpu_custom_call" | custom-call | tf_op jit(solution)/shard_map/pallas_call | solution.py:173
  17.0 13.1 %all-to-all-start = ((bf16[64,8,2432]{2,1,0:T(8,128)(2,1)}), bf16[64,8,2432]{2,1,0:T(8,128)(2,1)S(1)}, u32[]{:S(2)}, u32[]{:S(2)}) async-start(bf16[64,8,2432]{2,1,0:T(8,128)(2,1)} %bitcast.11), calls=%async_computation | async-start | bytes 4980736 | tf_op jit(solution)/shard_map/all_to_all | solution.py:178
  30.1 0.1 copy.37.slots_ref
  30.3 59.3 %all-to-all-done = bf16[64,8,2432]{2,1,0:T(8,128)(2,1)S(1)} async-done(((bf16[64,8,2432]{2,1,0:T(8,128)(2,1)}), bf16[64,8,2432]{2,1,0:T(8,128)(2,1)S(1)}, u32[]{:S(2)}, u32[]{:S(2)}) %all-to-all-start) | async-done | bytes 2490400 | tf_op jit(solution)/shard_map/all_to_all | solution.py:178
  89.6 1.4 copy-done.2
  91.0 7.0 %shard_map.122 = bf16[512,1792]{1,0:T(8,128)(2,1)} custom-call(s32[256,1]{1,0:T(8,128)S(1)} %copy.37.slots_ref, bf16[512,2432]{1,0:T(8,128)(2,1)} %bitcast.10), custom_call_target="tpu_custom_call" | custom-call | tf_op jit(solution)/shard_map/pallas_call | solution.py:194
  98.0 6.4 %all-to-all-start.1 = ((bf16[64,8,1792]{2,1,0:T(8,128)(2,1)}), bf16[64,8,1792]{2,1,0:T(8,128)(2,1)}, u32[]{:S(2)}, u32[]{:S(2)}) async-start(bf16[64,8,1792]{2,1,0:T(8,128)(2,1)} %bitcast.4), calls=%async_computation.1 | async-start | bytes 3670016 | tf_op jit(solution)/shard_map/all_to_all | solution.py:204
  104.5 0.1 reshape.66.rows_ref
  104.5 0.1 reshape.67.halves_ref
  104.6 0.1 copy.38
  104.8 20.8 %shard_map.123 = (bf16[640,1152]{1,0:T(8,128)(2,1)S(1)}, bf16[640,1152]{1,0:T(8,128)(2,1)S(1)}, bf16[640,1152]{1,0:T(8,128)(2,1)}) custom-call(s32[256,2]{1,0:T(8,128)S(1)} %bitcast.9, bf16[640,1152]{1,0:T(8,128)(2,1)} %q_ref.3, bf16[640,1152]{1,0:T(8,128)(2,1)} %k_ref.3, bf16[640,1152]{1,0:T(8,128)(2,1)} %v_ref.3, bf16[640,1152]{1,0:T(8,128)(2,1)} %g_ref.3, ...), custom_call_target="tpu_custom_call" | custom-call | tf_op jit(solution)/shard_map/pallas_call | solution.py:184
  125.6 24.0 %all-to-all-done.1 = bf16[64,8,1792]{2,1,0:T(8,128)(2,1)} async-done(((bf16[64,8,1792]{2,1,0:T(8,128)(2,1)}), bf16[64,8,1792]{2,1,0:T(8,128)(2,1)}, u32[]{:S(2)}, u32[]{:S(2)}) %all-to-all-start.1) | async-done | bytes 1835040 | tf_op jit(solution)/shard_map/all_to_all | solution.py:204
  149.6 6.2 %shard_map.124 = (bf16[640,1152]{1,0:T(8,128)(2,1)}, bf16[640,1152]{1,0:T(8,128)(2,1)}, bf16[640,1152]{1,0:T(8,128)(2,1)}) custom-call(s32[1,512]{1,0:T(1,128)S(1)} %reshape.66.rows_ref, s32[1,512]{1,0:T(1,128)S(1)} %reshape.67.halves_ref, bf16[512,1792]{1,0:T(8,128)(2,1)} %bitcast.5.back_ref, bf16[640,1152]{1,0:T(8,128)(2,1)S(1)} %get-tuple-element.6.lq_ref, ...), custom_call_target="tpu_custom_call" | custom-call | tf_op jit(solution)/shard_map/pallas_call | solution.py:208
  (16 shorter events, 0.2 us)
Async XLA Ops:
  5.6 1.4 copy-start
  7.0 1.4 copy-start.1
  17.0 13.1 %copy-start.6 = (s32[1,256]{1,0:T(1,128)S(1)}, s32[1,256]{1,0:T(1,128)}, u32[]{:S(2)}) copy-start(s32[1,256]{1,0:T(1,128)} %param.18) | copy-start | bytes 3076
  17.0 72.6 %all-to-all-start = ((bf16[64,8,2432]{2,1,0:T(8,128)(2,1)}), bf16[64,8,2432]{2,1,0:T(8,128)(2,1)S(1)}, u32[]{:S(2)}, u32[]{:S(2)}) async-start(bf16[64,8,2432]{2,1,0:T(8,128)(2,1)} %bitcast.11), calls=%async_computation | async-start | bytes 4980736 | tf_op jit(solution)/shard_map/all_to_all | solution.py:178
  89.6 1.4 copy-start.2
  98.0 6.6 %copy-start.5 = (s32[2,256]{1,0:T(2,128)S(1)}, s32[2,256]{1,0:T(2,128)}, u32[]{:S(2)}) copy-start(s32[2,256]{1,0:T(2,128)} %param.16) | copy-start | bytes 6148
  98.0 6.8 %copy-start.3 = (bf16[640,16]{0,1:T(8,128)(2,1)S(1)}, bf16[640,16]{0,1:T(8,128)(2,1)}, u32[]{:S(2)}) copy-start(bf16[640,16]{0,1:T(8,128)(2,1)} %param.14) | copy-start | bytes 61444
  98.0 6.8 %copy-start.4 = (bf16[640,16]{0,1:T(8,128)(2,1)S(1)}, bf16[640,16]{0,1:T(8,128)(2,1)}, u32[]{:S(2)}) copy-start(bf16[640,16]{0,1:T(8,128)(2,1)} %param.15) | copy-start | bytes 61444
  98.0 51.6 %all-to-all-start.1 = ((bf16[64,8,1792]{2,1,0:T(8,128)(2,1)}), bf16[64,8,1792]{2,1,0:T(8,128)(2,1)}, u32[]{:S(2)}, u32[]{:S(2)}) async-start(bf16[64,8,1792]{2,1,0:T(8,128)(2,1)} %bitcast.4), calls=%async_computation.1 | async-start | bytes 3670016 | tf_op jit(solution)/shard_map/all_to_all | solution.py:204
where the time goes:
time: 156 us
  waiting for transfers between devices  83.3 us (53%)
  Pallas kernels  42.6 us (27%)
  starting transfers between devices  19.6 us (13%)
  local copies, waits for them, and re-layouts  6.85 us (4%)
  other arithmetic  2.7 us (2%)
    all_to_all x1, waiting for transfers between devices, per_device(): lax.all_to_all(outgoing.reshape(devices, slot_cap, sent_width), 'ctx', sp...  59.3 us
    all_to_all x1, waiting for transfers between devices, per_device(): lax.all_to_all(replies.reshape(devices, slot_cap, back_width), 'ctx', spl...  24 us
    pallas_call x1, Pallas kernels, per_device(): pl.pallas_call(functools.partial(local_kernel, heads, size), out_shape=(w...  20.8 us
    all_to_all x1, starting transfers between devices, per_device(): lax.all_to_all(outgoing.reshape(devices, slot_cap, sent_width), 'ctx', sp...  13.1 us
    pallas_call x1, Pallas kernels, per_device(): pl.pallas_call(pack_kernel, out_shape=jax.ShapeDtypeStruct((slots, sent_w...  8.65 us
    pallas_call x1, Pallas kernels, per_device(): pl.pallas_call(functools.partial(cross_kernel, kept, size, half), out_sha...  6.99 us
    all_to_all x1, starting transfers between devices, per_device(): lax.all_to_all(replies.reshape(devices, slot_cap, back_width), 'ctx', spl...  6.44 us
    pallas_call x1, Pallas kernels, per_device(): pl.pallas_call(functools.partial(combine_kernel, half), out_shape=(whole,...  6.18 us
  transfers between devices with their start and end apart: 2, of which 2 were waited for; matrix products, arithmetic and copies ran while one was open for 0% of the time, Pallas kernels for 13%

commit v1 on v0

--- a/solution.py
+++ b/solution.py
@@ -8,7 +8,13 @@
 from jax.sharding import PartitionSpec as P
 
 LANES = 128
-PARAMS = pltpu.CompilerParams(vmem_limit_bytes=50 * 2**20)
+CODE = 1024
+
+
+def vmem(mebibytes):
+    return pltpu.CompilerParams(vmem_limit_bytes=mebibytes * 2**20)
+
+
 NT = (((1,), (1,)), ((), ()))
 TN = (((0,), (0,)), ((), ()))
 
@@ -80,26 +86,76 @@
                 out[...] += placed
 
 
-def pack_kernel(rows_ref, halves_ref, q_ref, v_ref, k_ref, g_ref, stats_ref, out_ref):
-    tokens, width = q_ref.shape
+def whole_product(dims, left, right):
+    high = (right >> 4).astype(jnp.float32).astype(jnp.bfloat16)
+    low = (right & 15).astype(jnp.float32).astype(jnp.bfloat16)
+    return dot(left, high, dims) * 16 + dot(left, low, dims)
+
+
+def pack_kernel(
+    slot_cap, owner_ref, send_ref, lse_ref, delta_ref, q_hbm, v_hbm, k_hbm, g_hbm, out_hbm, codes_ref, *scratch
+):
+    sources, out, in_sems, out_sems = scratch[:4], scratch[4], scratch[5], scratch[6]
+    loads = [
+        pltpu.make_async_copy(hbm, ref, in_sems.at[at])
+        for at, (hbm, ref) in enumerate(zip((q_hbm, v_hbm, k_hbm, g_hbm), sources))
+    ]
+    for load in loads:
+        load.start()
+    tokens, width = sources[0].shape
     half = width // 2
-    slots = out_ref.shape[0]
-    token = lax.broadcasted_iota(jnp.int32, (slots, tokens), 1)
-    named = rows_ref[...] == token
-    second = halves_ref[...] == 1
-    picks = [(named & ~second).astype(jnp.bfloat16), (named & second).astype(jnp.bfloat16)]
-    pieces = []
-    for ref in (q_ref, v_ref, k_ref, g_ref):
-        source = ref[...]
-        pieces.append((dot(picks[0], source[:, :half]) + dot(picks[1], source[:, half:])).astype(jnp.bfloat16))
-    stats = stats_ref[...]
-    kept = stats.shape[1] // 2
-    pieces.append((dot(picks[0], stats[:, :kept]) + dot(picks[1], stats[:, kept:])).astype(jnp.bfloat16))
-    pieces.append(jnp.zeros((slots, out_ref.shape[1] - 4 * half - kept), jnp.bfloat16))
-    out_ref[...] = jnp.concatenate(pieces, 1)
-
-
-def cross_kernel(heads, size, half, slots_ref, arrived_ref, out_ref, rows, sums, stat_rows):
+    slots, sent_width = out.shape
+    devices = owner_ref.shape[1]
+
+    def grid(rows, columns, axis):
+        return lax.broadcasted_iota(jnp.int32, (rows, columns), axis)
+
+    def ones(mask):
+        return jnp.where(mask, 1.0, 0.0).astype(jnp.bfloat16)
+
+    place = ones(owner_ref[...] == grid(devices, devices, 0))
+    even = ones(grid(devices, devices, 1) == (grid(devices, devices, 0) & ~1))
+    spread = ones(grid(slots, devices, 0) // slot_cap == grid(slots, devices, 1))
+    placed = dot(spread, place).astype(jnp.bfloat16)
+    first = dot(placed, even).astype(jnp.bfloat16)
+    owners = dot(first, place, NT).astype(jnp.bfloat16)
+    rows = whole_product(NT, owners, send_ref[...])
+    second = dot(placed, ones((grid(devices, slot_cap, 0) & 1) == 1))
+    own_slot = (grid(slots, slot_cap, 0) & (slot_cap - 1)) == grid(slots, slot_cap, 1)
+    codes = jnp.sum(jnp.where(own_slot, rows + second * CODE, 0.0), 1, keepdims=True)
+    codes_ref[...] = jnp.broadcast_to(codes, (slots, LANES)).T[: codes_ref.shape[0]].astype(jnp.int32)
+    codes = codes.astype(jnp.int32)
+    token = grid(slots, tokens, 1)
+    picks = ones(codes == token), ones(codes - CODE == token)
+
+    kept = lse_ref.shape[0] // 2
+    stats = jnp.zeros((slots, 2 * kept), jnp.float32)
+    for part, pick in enumerate(picks):
+        lines = jnp.concatenate(
+            [lse_ref[part * kept : (part + 1) * kept], delta_ref[part * kept : (part + 1) * kept]], 0
+        )
+        stats += dot(pick, lines, NT)
+    fill = jnp.zeros((slots, sent_width - 4 * half - 2 * kept), jnp.float32)
+    out[:, 4 * half :] = jnp.concatenate([stats, fill], 1).astype(jnp.bfloat16)
+    spans = (0, width, 2 * width, sent_width)
+    stores = [
+        pltpu.make_async_copy(out.at[:, low:high], out_hbm.at[:, low:high], out_sems.at[at])
+        for at, (low, high) in enumerate(zip(spans, spans[1:]))
+    ]
+    stores[2].start()
+    for at in range(2):
+        loads[2 * at].wait()
+        loads[2 * at + 1].wait()
+        one, two = sources[2 * at], sources[2 * at + 1]
+        total = dot(picks[0], jnp.concatenate([one[:, :half], two[:, :half]], 1))
+        total += dot(picks[1], jnp.concatenate([one[:, half:], two[:, half:]], 1))
+        out[:, spans[at] : spans[at + 1]] = total.astype(jnp.bfloat16)
+        stores[at].start()
+    for store in stores:
+        store.wait()
+
+
+def cross_kernel(heads, size, half, slots_ref, arrived_ref, out_hbm, rows, sums, stat_rows, out, sems):
     win, count = slots_ref.shape[0], arrived_ref.shape[0]
     picker = (slots_ref[...] == lax.broadcasted_iota(jnp.int32, (win, count), 1)).astype(jnp.bfloat16)
     picked = dot(picker, arrived_ref[...])
@@ -119,16 +175,25 @@
         (sums, 2 * half),
         (sums, half),
     )
-    out_ref[...] = dot(picker, sums[...].astype(jnp.bfloat16), TN).astype(jnp.bfloat16)
-
-
-def combine_kernel(half, rows_ref, halves_ref, back_ref, lq_ref, lk_ref, lv_ref, dq_ref, dk_ref, dv_ref):
-    tokens, slots = lq_ref.shape[0], back_ref.shape[0]
-    named = rows_ref[...] == lax.broadcasted_iota(jnp.int32, (tokens, slots), 0)
-    second = halves_ref[...] == 1
-    placers = [(named & ~second).astype(jnp.bfloat16), (named & second).astype(jnp.bfloat16)]
+    middle = up(half)
+    stores = []
+    for at, (low, high) in enumerate(((0, middle), (middle, out.shape[1]))):
+        out[:, low:high] = dot(picker, sums[:, low:high].astype(jnp.bfloat16), TN).astype(jnp.bfloat16)
+        stores.append(pltpu.make_async_copy(out.at[:, low:high], out_hbm.at[:, low:high], sems.at[at]))
+        stores[at].start()
+    for store in stores:
+        store.wait()
+
+
+def combine_kernel(half, codes_ref, back_ref, lq_ref, lk_ref, lv_ref, dq_ref, dk_ref, dv_ref):
+    count, slots = lq_ref.shape[0], back_ref.shape[0]
+    token = lax.broadcasted_iota(jnp.int32, (count, slots), 0) + pl.program_id(0) * count
+    codes = codes_ref[:1]
     back = back_ref[...]
-    parts = [dot(placer, back).astype(jnp.bfloat16) for placer in placers]
+    parts = [
+        dot(jnp.where(codes - at * CODE == token, 1.0, 0.0).astype(jnp.bfloat16), back).astype(jnp.bfloat16)
+        for at in range(2)
+    ]
     for at, (local, out) in enumerate(((lq_ref, dq_ref), (lv_ref, dv_ref), (lk_ref, dk_ref))):
         both = [part[:, at * half : (at + 1) * half] for part in parts]
         out[...] = local[...] + jnp.concatenate(both, 1)
@@ -155,31 +220,25 @@
     slots = devices * slot_cap
     bf16, f32 = jnp.bfloat16, jnp.float32
 
-    peers = jnp.arange(devices, dtype=jnp.int32)
-    named = window_owner[None, :] == peers[:, None]
-    first_of_pair = jnp.repeat(window_owner[::2], 2)
-    pair_owner = jnp.sum(jnp.where(named, first_of_pair[None, :], 0), 1)
-    half_ids = jnp.sum(jnp.where(named, (peers % 2)[None, :], 0), 1)
-    half_rows = jnp.sum(jnp.where((pair_owner[:, None] == peers[None, :])[:, :, None], send_rows[0][None], 0), 1)
-    half_ids = jnp.broadcast_to(half_ids[:, None], (devices, slot_cap))
-    row_col, half_col = half_rows.reshape(slots, 1), half_ids.reshape(slots, 1)
-    row_row, half_row = half_rows.reshape(1, slots), half_ids.reshape(1, slots)
-
     kept = heads // 2
-    stat_cols = jnp.concatenate(
-        [logsumexp[:, :kept], row_delta[:, :kept], logsumexp[:, kept:], row_delta[:, kept:]], 1
-    )
+    lse_lines, delta_lines = logsumexp.T, row_delta.T
     sent_width = up(4 * half + heads)
-    outgoing = pl.pallas_call(
-        pack_kernel,
-        out_shape=jax.ShapeDtypeStruct((slots, sent_width), bf16),
-        compiler_params=PARAMS,
-    )(row_col, half_col, query_rows, value_rows, key_rows, out_grad, stat_cols)
+    far = pl.BlockSpec(memory_space=pltpu.HBM)
+    inside = pl.BlockSpec(memory_space=pltpu.VMEM)
+    outgoing, codes = pl.pallas_call(
+        functools.partial(pack_kernel, slot_cap),
+        out_shape=(jax.ShapeDtypeStruct((slots, sent_width), bf16), jax.ShapeDtypeStruct((8, slots), jnp.int32)),
+        in_specs=[inside] * 4 + [far] * 4,
+        out_specs=(far, inside),
+        scratch_shapes=[pltpu.VMEM((tokens, width), bf16)] * 4
+        + [pltpu.VMEM((slots, sent_width), bf16), pltpu.SemaphoreType.DMA((4,)), pltpu.SemaphoreType.DMA((3,))],
+        compiler_params=vmem(62),
+    )(window_owner.reshape(1, devices), send_rows[0].T, lse_lines, delta_lines, query_rows, value_rows, key_rows, out_grad)
     arrived = lax.all_to_all(
         outgoing.reshape(devices, slot_cap, sent_width), "ctx", split_axis=0, concat_axis=0, tiled=True
     ).reshape(slots, sent_width)
 
-    stat_lines = jnp.concatenate([logsumexp, row_delta], 1).T
+    stat_lines = jnp.concatenate([lse_lines, delta_lines], 0)
     whole = jax.ShapeDtypeStruct((tokens, width), bf16)
     local = pl.pallas_call(
         functools.partial(local_kernel, heads, size),
@@ -187,7 +246,7 @@
         scratch_shapes=[pltpu.VMEM((win, width), bf16)] * 4
         + [pltpu.VMEM((win, width), f32)] * 3
         + [pltpu.VMEM((2 * heads, win), f32)],
-        compiler_params=PARAMS,
+        compiler_params=vmem(62),
     )(local_members.T, query_rows, key_rows, value_rows, out_grad, stat_lines)
 
     back_width = up(3 * half)
@@ -198,18 +257,28 @@
             pltpu.VMEM((win, sent_width), bf16),
             pltpu.VMEM((win, back_width), f32),
             pltpu.VMEM((sent_width - 4 * half, win), f32),
+            pltpu.VMEM((slots, back_width), bf16),
+            pltpu.SemaphoreType.DMA((2,)),
         ],
-        compiler_params=PARAMS,
+        out_specs=far,
+        compiler_params=vmem(32),
     )(window_slots.reshape(win, 1), arrived)
     returned = lax.all_to_all(
         replies.reshape(devices, slot_cap, back_width), "ctx", split_axis=0, concat_axis=0, tiled=True
     ).reshape(slots, back_width)
 
+    block = LANES
+    some = pl.BlockSpec((block, width), lambda at: (at, 0))
     return pl.pallas_call(
         functools.partial(combine_kernel, half),
         out_shape=(whole,) * 3,
-        compiler_params=PARAMS,
-    )(row_row, half_row, returned, *local)
+        grid=(tokens // block,),
+        in_specs=[pl.BlockSpec((8, slots), lambda at: (0, 0)), pl.BlockSpec((slots, back_width), lambda at: (0, 0))]
+        + [some] * 3,
+        out_specs=(some,) * 3,
+        input_output_aliases={2: 0, 3: 1, 4: 2},
+        compiler_params=vmem(32),
+    )(codes, returned, *local)
 
 
 def solution(mesh):

time: 156 us -> 147 us (0.942)
  local copies, waits for them, and re-layouts: 6.85 us -> 2.2 us
  other arithmetic: 2.7 us -> 0.62 us
  Pallas kernels: 42.6 us -> 41 us
    reduce_sum x2 -> x0, other arithmetic: 2.61 us -> none  [the longest x1 1.85 us: per_device(): jnp.sum(jnp.where((pair_owner[:, None] == peers[None, :])[:, :, None], se...]
    pallas_call x1, Pallas kernels: 6.99 us -> 4.41 us  [per_device(): pl.pallas_call(functools.partial(cross_kernel, kept, size, half), out_sha...]
    unnamed x15 -> x13, local copies, waits for them, and re-layouts: 4.32 us -> 2.07 us
  transfers between devices with their start and end apart: 2 -> 2, of which waited for: 2 -> 2; matrix products, arithmetic and copies ran while one was open for 0% -> 1% of each run, Pallas kernels for 13% -> 14%
where the time goes in v1:
time: 147 us; the launch traced here: 146 us
  waiting for transfers between devices  82.3 us (56%)
  Pallas kernels  41 us (28%)
  starting transfers between devices  19.3 us (13%)
  local copies, waits for them, and re-layouts  2.2 us (1%)
    all_to_all x1, waiting for transfers between devices, per_device(): lax.all_to_all(outgoing.reshape(devices, slot_cap, sent_width), 'ctx', sp...  59.3 us
    all_to_all x1, waiting for transfers between devices, per_device(): lax.all_to_all(replies.reshape(devices, slot_cap, back_width), 'ctx', spl...  23 us
    pallas_call x1, Pallas kernels, per_device(): pl.pallas_call(functools.partial(local_kernel, heads, size), out_shape=(w...  20.8 us
    all_to_all x1, starting transfers between devices, per_device(): lax.all_to_all(outgoing.reshape(devices, slot_cap, sent_width), 'ctx', sp...  13 us
    pallas_call x1, Pallas kernels, per_device(): pl.pallas_call(functools.partial(pack_kernel, slot_cap), out_shape=(jax.S...  8.85 us
    pallas_call x1, Pallas kernels, per_device(): pl.pallas_call(functools.partial(combine_kernel, half), out_shape=(whole,...  6.88 us
    all_to_all x1, starting transfers between devices, per_device(): lax.all_to_all(replies.reshape(devices, slot_cap, back_width), 'ctx', spl...  6.28 us
    pallas_call x1, Pallas kernels, per_device(): pl.pallas_call(functools.partial(cross_kernel, kept, size, half), out_sha...  4.41 us
  transfers between devices with their start and end apart: 2, of which 2 were waited for; matrix products, arithmetic and copies ran while one was open for 1% of the time, Pallas kernels for 14%

profile of v1, /device:TPU:1, one launch (start us, length us, event | category | flops | bytes accessed | tf_op | source)
XLA Modules:
  0.0 146.0 jit_solution(12622758893793868796)
XLA Ops:
  0.6 8.8 %shard_map.121 = (bf16[512,2432]{1,0:T(8,128)(2,1)}, s32[8,512]{1,0:T(8,128)}) custom-call(s32[1,64]{1,0:T(1,128)} %bitcast.23, s32[8,64]{1,0:T(8,128)} %bitcast.21, bf16[16,640]{1,0:T(8,128)(2,1)} %bitcast.17, bf16[16,640]{1,0:T(8,128)(2,1)} %bitcast.19, bf16[640,1152]{1,0:T(8,128)(2,1)} %q_ref.1, bf16[640,1152]{1,0:T(8,128)(2,1)} %v_ref.1, ...), custom_call_target="tpu_custom_call" | custom-call | tf_op jit(solution)/shard_map/pallas_call | solution.py:228
  9.5 0.0 copy-start.5
  9.5 13.0 %all-to-all-start = ((bf16[64,8,2432]{2,1,0:T(8,128)(2,1)}), bf16[64,8,2432]{2,1,0:T(8,128)(2,1)S(1)}, u32[]{:S(2)}, u32[]{:S(2)}) async-start(bf16[64,8,2432]{2,1,0:T(8,128)(2,1)} %bitcast.15), calls=%async_computation | async-start | bytes 4980736 | tf_op jit(solution)/shard_map/all_to_all | solution.py:237
  22.5 0.0 copy-done.5
  22.5 0.1 copy.17.slots_ref
  22.7 59.3 %all-to-all-done = bf16[64,8,2432]{2,1,0:T(8,128)(2,1)S(1)} async-done(((bf16[64,8,2432]{2,1,0:T(8,128)(2,1)}), bf16[64,8,2432]{2,1,0:T(8,128)(2,1)S(1)}, u32[]{:S(2)}, u32[]{:S(2)}) %all-to-all-start) | async-done | bytes 2490400 | tf_op jit(solution)/shard_map/all_to_all | solution.py:237
  82.0 4.4 %shard_map.122 = bf16[512,1792]{1,0:T(8,128)(2,1)S(1)} custom-call(s32[256,1]{1,0:T(8,128)S(1)} %copy.17.slots_ref, bf16[512,2432]{1,0:T(8,128)(2,1)S(1)} %bitcast.12), custom_call_target="tpu_custom_call" | custom-call | tf_op jit(solution)/shard_map/pallas_call | solution.py:253
  86.4 0.0 copy-start
  86.4 1.2 copy-done
  87.6 0.0 copy-start.4
  87.6 0.0 copy-start.2
  87.6 0.0 copy-start.3
  87.6 6.3 %all-to-all-start.1 = ((bf16[64,8,1792]{2,1,0:T(8,128)(2,1)}), bf16[64,8,1792]{2,1,0:T(8,128)(2,1)S(1)}, u32[]{:S(2)}, u32[]{:S(2)}) async-start(bf16[64,8,1792]{2,1,0:T(8,128)(2,1)} %bitcast.14), calls=%async_computation.1 | async-start | bytes 3670016 | tf_op jit(solution)/shard_map/all_to_all | solution.py:266
  93.9 0.0 copy-done.4
  93.9 0.8 copy.18
  94.7 0.0 copy-done.2
  94.7 0.0 copy-done.3
  94.7 0.6 pad_maximum_fusion.stats_ref
  95.4 0.0 copy-start.1
  95.4 20.8 %shard_map.123 = (bf16[640,1152]{1,0:T(8,128)(2,1)}, bf16[640,1152]{1,0:T(8,128)(2,1)}, bf16[640,1152]{1,0:T(8,128)(2,1)}) custom-call(s32[256,2]{1,0:T(8,128)} %bitcast.16, bf16[640,1152]{1,0:T(8,128)(2,1)} %q_ref.1, bf16[640,1152]{1,0:T(8,128)(2,1)} %k_ref.1, bf16[640,1152]{1,0:T(8,128)(2,1)} %v_ref.1, bf16[640,1152]{1,0:T(8,128)(2,1)} %g_ref.1, ...), custom_call_target="tpu_custom_call" | custom-call | tf_op jit(solution)/shard_map/pallas_call | solution.py:243
  116.2 23.0 %all-to-all-done.1 = bf16[64,8,1792]{2,1,0:T(8,128)(2,1)S(1)} async-done(((bf16[64,8,1792]{2,1,0:T(8,128)(2,1)}), bf16[64,8,1792]{2,1,0:T(8,128)(2,1)S(1)}, u32[]{:S(2)}, u32[]{:S(2)}) %all-to-all-start.1) | async-done | bytes 1835040 | tf_op jit(solution)/shard_map/all_to_all | solution.py:266
  139.2 0.0 copy-done.1
  139.2 6.9 %shard_map.124 = (bf16[640,1152]{1,0:T(8,128)(2,1)}, bf16[640,1152]{1,0:T(8,128)(2,1)}, bf16[640,1152]{1,0:T(8,128)(2,1)}) custom-call(s32[8,512]{1,0:T(8,128)S(1)} %copy-done.1, bf16[512,1792]{1,0:T(8,128)(2,1)S(1)} %bitcast.13, bf16[640,1152]{1,0:T(8,128)(2,1)} %get-tuple-element.10.lq_ref, ...), custom_call_target="tpu_custom_call", output_to_operand_aliasing={{0}: (2, {}), {1}: (3, {}), {2}: (4, {})} | custom-call | tf_op jit(solution)/shard_map/pallas_call | solution.py:272
Async XLA Ops:
  9.5 13.0 %copy-start.5 = (s32[1,256]{1,0:T(1,128)S(1)}, s32[1,256]{1,0:T(1,128)}, u32[]{:S(2)}) copy-start(s32[1,256]{1,0:T(1,128)} %param.18) | copy-start | bytes 3076
  9.5 72.5 %all-to-all-start = ((bf16[64,8,2432]{2,1,0:T(8,128)(2,1)}), bf16[64,8,2432]{2,1,0:T(8,128)(2,1)S(1)}, u32[]{:S(2)}, u32[]{:S(2)}) async-start(bf16[64,8,2432]{2,1,0:T(8,128)(2,1)} %bitcast.15), calls=%async_computation | async-start | bytes 4980736 | tf_op jit(solution)/shard_map/all_to_all | solution.py:237
  86.4 1.3 copy-start
  87.6 6.3 %copy-start.4 = (s32[2,256]{1,0:T(2,128)S(1)}, s32[2,256]{1,0:T(2,128)}, u32[]{:S(2)}) copy-start(s32[2,256]{1,0:T(2,128)} %param.16) | copy-start | bytes 6148
  87.6 7.1 %copy-start.2 = (bf16[640,16]{0,1:T(8,128)(2,1)S(1)}, bf16[640,16]{0,1:T(8,128)(2,1)}, u32[]{:S(2)}) copy-start(bf16[640,16]{0,1:T(8,128)(2,1)} %param.14) | copy-start | bytes 61444
  87.6 7.1 %copy-start.3 = (bf16[640,16]{0,1:T(8,128)(2,1)S(1)}, bf16[640,16]{0,1:T(8,128)(2,1)}, u32[]{:S(2)}) copy-start(bf16[640,16]{0,1:T(8,128)(2,1)} %param.15) | copy-start | bytes 61444
  87.6 51.5 %all-to-all-start.1 = ((bf16[64,8,1792]{2,1,0:T(8,128)(2,1)}), bf16[64,8,1792]{2,1,0:T(8,128)(2,1)S(1)}, u32[]{:S(2)}, u32[]{:S(2)}) async-start(bf16[64,8,1792]{2,1,0:T(8,128)(2,1)} %bitcast.14), calls=%async_computation.1 | async-start | bytes 3670016 | tf_op jit(solution)/shard_map/all_to_all | solution.py:266
  95.4 43.8 %copy-start.1 = (s32[8,512]{1,0:T(8,128)S(1)}, s32[8,512]{1,0:T(8,128)}, u32[]{:S(2)}) copy-start(s32[8,512]{1,0:T(8,128)} %get-tuple-element.8.codes_ref) | copy-start | bytes 49156

commit v2 on v0

--- a/solution.py
+++ b/solution.py
@@ -8,7 +8,13 @@
 from jax.sharding import PartitionSpec as P
 
 LANES = 128
-PARAMS = pltpu.CompilerParams(vmem_limit_bytes=50 * 2**20)
+CODE = 1024
+
+
+def vmem(mebibytes):
+    return pltpu.CompilerParams(vmem_limit_bytes=mebibytes * 2**20)
+
+
 NT = (((1,), (1,)), ((), ()))
 TN = (((0,), (0,)), ((), ()))
 
@@ -80,23 +86,112 @@
                 out[...] += placed
 
 
-def pack_kernel(rows_ref, halves_ref, q_ref, v_ref, k_ref, g_ref, stats_ref, out_ref):
-    tokens, width = q_ref.shape
+def whole_product(dims, left, right):
+    high = (right >> 4).astype(jnp.float32).astype(jnp.bfloat16)
+    low = (right & 15).astype(jnp.float32).astype(jnp.bfloat16)
+    return dot(left, high, dims) * 16 + dot(left, low, dims)
+
+
+def iota(rows, columns, axis):
+    return lax.broadcasted_iota(jnp.int32, (rows, columns), axis)
+
+
+def ones(mask):
+    return jnp.where(mask, 1.0, 0.0).astype(jnp.bfloat16)
+
+
+def codes_kernel(slot_cap, owner_ref, send_ref, codes_ref):
+    devices, slots = owner_ref.shape[1], codes_ref.shape[1]
+    place = ones(owner_ref[...] == iota(devices, devices, 0))
+    even = ones(iota(devices, devices, 1) == (iota(devices, devices, 0) & ~1))
+    spread = ones(iota(slots, devices, 0) // slot_cap == iota(slots, devices, 1))
+    placed = dot(spread, place).astype(jnp.bfloat16)
+    first = dot(placed, even).astype(jnp.bfloat16)
+    owners = dot(first, place, NT).astype(jnp.bfloat16)
+    rows = whole_product(NT, owners, send_ref[...])
+    second = dot(placed, ones((iota(devices, slot_cap, 0) & 1) == 1))
+    own_slot = (iota(slots, slot_cap, 0) & (slot_cap - 1)) == iota(slots, slot_cap, 1)
+    codes = jnp.sum(jnp.where(own_slot, rows + second * CODE, 0.0), 1, keepdims=True)
+    codes_ref[...] = jnp.broadcast_to(codes, (slots, LANES)).T[: codes_ref.shape[0]].astype(jnp.int32)
+
+
+def pack_kernel(slot_cap, owner_hbm, send_hbm, lse_hbm, delta_hbm, q_hbm, v_hbm, k_hbm, g_hbm, out_hbm, *scratch):
+    owner, send, lse, delta = scratch[:4]
+    sources, order, starts, ranked, out, in_sems, out_sems = scratch[4:8], *scratch[8:]
+    loads = [
+        pltpu.make_async_copy(hbm, ref, in_sems.at[at])
+        for at, (hbm, ref) in enumerate(
+            (
+                (owner_hbm, owner),
+                (send_hbm, send),
+                (owner_hbm, order),
+                *zip((q_hbm, v_hbm), sources),
+                (lse_hbm, lse),
+                (delta_hbm, delta),
+                *zip((k_hbm, g_hbm), sources[2:]),
+            )
+        )
+    ]
+    for load in loads:
+        load.start()
+    tokens, width = sources[0].shape
     half = width // 2
-    slots = out_ref.shape[0]
-    token = lax.broadcasted_iota(jnp.int32, (slots, tokens), 1)
-    named = rows_ref[...] == token
-    second = halves_ref[...] == 1
-    picks = [(named & ~second).astype(jnp.bfloat16), (named & second).astype(jnp.bfloat16)]
-    pieces = []
-    for ref in (q_ref, v_ref, k_ref, g_ref):
-        source = ref[...]
-        pieces.append((dot(picks[0], source[:, :half]) + dot(picks[1], source[:, half:])).astype(jnp.bfloat16))
-    stats = stats_ref[...]
-    kept = stats.shape[1] // 2
-    pieces.append((dot(picks[0], stats[:, :kept]) + dot(picks[1], stats[:, kept:])).astype(jnp.bfloat16))
-    pieces.append(jnp.zeros((slots, out_ref.shape[1] - 4 * half - kept), jnp.bfloat16))
-    out_ref[...] = jnp.concatenate(pieces, 1)
+    slots, sent_width = out.shape
+    devices = owner.shape[1]
+    pair_rows = slots // 2
+
+    loads[0].wait()
+    loads[1].wait()
+    place = ones(owner[...] == iota(devices, devices, 0))
+    spread = ones(iota(pair_rows, devices, 0) // slot_cap * 2 == iota(pair_rows, devices, 1))
+    owners = dot(spread, place, NT).astype(jnp.bfloat16)
+    rows = whole_product(NT, owners, send[...])
+    own_slot = (iota(pair_rows, slot_cap, 0) & (slot_cap - 1)) == iota(pair_rows, slot_cap, 1)
+    rows = jnp.sum(jnp.where(own_slot, rows, 0.0), 1, keepdims=True).astype(jnp.int32)
+    pick = ones(rows == iota(pair_rows, tokens, 1))
+
+    loads[2].wait()
+    for at in range(devices):
+        starts[order[0, at]] = (at & 1) * pair_rows + at // 2 * slot_cap
+
+    kept = lse.shape[0] // 2
+    spans = (0, width, 2 * width, sent_width)
+    stores = [
+        pltpu.make_async_copy(out.at[:, low:high], out_hbm.at[:, low:high], out_sems.at[at])
+        for at, (low, high) in enumerate(zip(spans, spans[1:]))
+    ]
+
+    def deliver(at):
+        span = slice(spans[at], spans[at + 1])
+        for device in range(0, devices, 2):
+            both = [
+                ranked[pl.ds(pl.multiple_of(starts[device + core] & (slots - slot_cap), slot_cap), slot_cap), span]
+                for core in range(2)
+            ]
+            out[device * slot_cap : (device + 2) * slot_cap, span] = jnp.concatenate(both, 0).astype(jnp.bfloat16)
+        stores[at].start()
+
+    for at in range(2):
+        loads[3 + 4 * at].wait()
+        loads[4 + 4 * at].wait()
+        one, two = sources[2 * at], sources[2 * at + 1]
+        for part in range(2):
+            cut = slice(part * half, (part + 1) * half)
+            ranked[part * pair_rows : (part + 1) * pair_rows, spans[at] : spans[at + 1]] = dot(
+                pick, jnp.concatenate([one[:, cut], two[:, cut]], 1)
+            )
+        deliver(at)
+        if at == 0:
+            loads[5].wait()
+            loads[6].wait()
+            for part in range(2):
+                cut = slice(part * kept, (part + 1) * kept)
+                stats = dot(pick, jnp.concatenate([lse[cut], delta[cut]], 0), NT)
+                fill = jnp.zeros((pair_rows, sent_width - spans[2] - 2 * kept), jnp.float32)
+                ranked[part * pair_rows : (part + 1) * pair_rows, spans[2] :] = jnp.concatenate([stats, fill], 1)
+            deliver(2)
+    for store in stores:
+        store.wait()
 
 
 def cross_kernel(heads, size, half, slots_ref, arrived_ref, out_ref, rows, sums, stat_rows):
@@ -122,16 +217,38 @@
     out_ref[...] = dot(picker, sums[...].astype(jnp.bfloat16), TN).astype(jnp.bfloat16)
 
 
-def combine_kernel(half, rows_ref, halves_ref, back_ref, lq_ref, lk_ref, lv_ref, dq_ref, dk_ref, dv_ref):
-    tokens, slots = lq_ref.shape[0], back_ref.shape[0]
-    named = rows_ref[...] == lax.broadcasted_iota(jnp.int32, (tokens, slots), 0)
-    second = halves_ref[...] == 1
-    placers = [(named & ~second).astype(jnp.bfloat16), (named & second).astype(jnp.bfloat16)]
+def combine_kernel(
+    half, codes_ref, back_ref, lq_hbm, lv_hbm, lk_hbm, dq_hbm, dv_hbm, dk_hbm, *scratch
+):
+    totals, in_sems, out_sems = scratch[:3], scratch[3], scratch[4]
+    blocks = in_sems.shape[1]
+    count, slots = totals[0].shape[0] // blocks, back_ref.shape[0]
+    spans = [slice(at * count, (at + 1) * count) for at in range(blocks)]
+
+    def copies(sources, targets, sems):
+        return [
+            [
+                pltpu.make_async_copy(source.at[span], target.at[span], sems.at[which, at])
+                for which, (source, target) in enumerate(zip(sources, targets))
+            ]
+            for at, span in enumerate(spans)
+        ]
+
+    loads = copies((lq_hbm, lv_hbm, lk_hbm), totals, in_sems)
+    stores = copies(totals, (dq_hbm, dv_hbm, dk_hbm), out_sems)
+    for load in sum(loads, []):
+        load.start()
     back = back_ref[...]
-    parts = [dot(placer, back).astype(jnp.bfloat16) for placer in placers]
-    for at, (local, out) in enumerate(((lq_ref, dq_ref), (lv_ref, dv_ref), (lk_ref, dk_ref))):
-        both = [part[:, at * half : (at + 1) * half] for part in parts]
-        out[...] = local[...] + jnp.concatenate(both, 1)
+    for at, span in enumerate(spans):
+        token = iota(count, slots, 0) + at * count
+        parts = [dot(ones(codes_ref[:1] - part * CODE == token), back).astype(jnp.bfloat16) for part in range(2)]
+        for which, total in enumerate(totals):
+            both = [part[:, which * half : (which + 1) * half] for part in parts]
+            loads[at][which].wait()
+            total[span] += jnp.concatenate(both, 1)
+            stores[at][which].start()
+    for store in sum(stores, []):
+        store.wait()
 
 
 def per_device(
@@ -155,31 +272,39 @@
     slots = devices * slot_cap
     bf16, f32 = jnp.bfloat16, jnp.float32
 
-    peers = jnp.arange(devices, dtype=jnp.int32)
-    named = window_owner[None, :] == peers[:, None]
-    first_of_pair = jnp.repeat(window_owner[::2], 2)
-    pair_owner = jnp.sum(jnp.where(named, first_of_pair[None, :], 0), 1)
-    half_ids = jnp.sum(jnp.where(named, (peers % 2)[None, :], 0), 1)
-    half_rows = jnp.sum(jnp.where((pair_owner[:, None] == peers[None, :])[:, :, None], send_rows[0][None], 0), 1)
-    half_ids = jnp.broadcast_to(half_ids[:, None], (devices, slot_cap))
-    row_col, half_col = half_rows.reshape(slots, 1), half_ids.reshape(slots, 1)
-    row_row, half_row = half_rows.reshape(1, slots), half_ids.reshape(1, slots)
-
     kept = heads // 2
-    stat_cols = jnp.concatenate(
-        [logsumexp[:, :kept], row_delta[:, :kept], logsumexp[:, kept:], row_delta[:, kept:]], 1
-    )
+    lse_lines, delta_lines = logsumexp.T, row_delta.T
     sent_width = up(4 * half + heads)
+    far = pl.BlockSpec(memory_space=pltpu.HBM)
+    inside = pl.BlockSpec(memory_space=pltpu.VMEM)
+    owner_line, send_lines = window_owner.reshape(1, devices), send_rows[0].T
     outgoing = pl.pallas_call(
-        pack_kernel,
+        functools.partial(pack_kernel, slot_cap),
         out_shape=jax.ShapeDtypeStruct((slots, sent_width), bf16),
-        compiler_params=PARAMS,
-    )(row_col, half_col, query_rows, value_rows, key_rows, out_grad, stat_cols)
+        in_specs=[far] * 8,
+        out_specs=far,
+        scratch_shapes=[
+            pltpu.VMEM((1, devices), jnp.int32),
+            pltpu.VMEM((slot_cap, devices), jnp.int32),
+            pltpu.VMEM((heads, tokens), bf16),
+            pltpu.VMEM((heads, tokens), bf16),
+        ]
+        + [pltpu.VMEM((tokens, width), bf16)] * 4
+        + [
+            pltpu.SMEM((1, devices), jnp.int32),
+            pltpu.SMEM((devices,), jnp.int32),
+            pltpu.VMEM((slots, sent_width), f32),
+            pltpu.VMEM((slots, sent_width), bf16),
+            pltpu.SemaphoreType.DMA((9,)),
+            pltpu.SemaphoreType.DMA((3,)),
+        ],
+        compiler_params=vmem(62),
+    )(owner_line, send_lines, lse_lines, delta_lines, query_rows, value_rows, key_rows, out_grad)
     arrived = lax.all_to_all(
         outgoing.reshape(devices, slot_cap, sent_width), "ctx", split_axis=0, concat_axis=0, tiled=True
     ).reshape(slots, sent_width)
 
-    stat_lines = jnp.concatenate([logsumexp, row_delta], 1).T
+    stat_lines = jnp.concatenate([lse_lines, delta_lines], 0)
     whole = jax.ShapeDtypeStruct((tokens, width), bf16)
     local = pl.pallas_call(
         functools.partial(local_kernel, heads, size),
@@ -187,7 +312,7 @@
         scratch_shapes=[pltpu.VMEM((win, width), bf16)] * 4
         + [pltpu.VMEM((win, width), f32)] * 3
         + [pltpu.VMEM((2 * heads, win), f32)],
-        compiler_params=PARAMS,
+        compiler_params=vmem(62),
     )(local_members.T, query_rows, key_rows, value_rows, out_grad, stat_lines)
 
     back_width = up(3 * half)
@@ -199,17 +324,28 @@
             pltpu.VMEM((win, back_width), f32),
             pltpu.VMEM((sent_width - 4 * half, win), f32),
         ],
-        compiler_params=PARAMS,
+        compiler_params=vmem(32),
     )(window_slots.reshape(win, 1), arrived)
     returned = lax.all_to_all(
         replies.reshape(devices, slot_cap, back_width), "ctx", split_axis=0, concat_axis=0, tiled=True
     ).reshape(slots, back_width)
 
-    return pl.pallas_call(
+    codes = pl.pallas_call(
+        functools.partial(codes_kernel, slot_cap),
+        out_shape=jax.ShapeDtypeStruct((8, slots), jnp.int32),
+        compiler_params=vmem(32),
+    )(owner_line, send_lines)
+    blocks = 2
+    dq, dv, dk = pl.pallas_call(
         functools.partial(combine_kernel, half),
         out_shape=(whole,) * 3,
-        compiler_params=PARAMS,
-    )(row_row, half_row, returned, *local)
+        in_specs=[inside] * 2 + [far] * 3,
+        out_specs=(far,) * 3,
+        scratch_shapes=[pltpu.VMEM((tokens, width), bf16)] * 3 + [pltpu.SemaphoreType.DMA((3, blocks))] * 2,
+        input_output_aliases={2: 0, 3: 1, 4: 2},
+        compiler_params=vmem(32),
+    )(codes, returned, local[0], local[2], local[1])
+    return dq, dk, dv
 
 
 def solution(mesh):

time: 156 us -> 142 us (0.910)
  Pallas kernels: 42.6 us -> 37.3 us
  local copies, waits for them, and re-layouts: 6.85 us -> 2.22 us
  other arithmetic: 2.7 us -> 0.62 us
  waiting for transfers between devices: 83.3 us -> 81.5 us
    pallas_call x1, Pallas kernels: 6.99 us -> 4.03 us  [per_device(): pl.pallas_call(functools.partial(cross_kernel, kept, size, half), out_sha...]
    reduce_sum x2 -> x0, other arithmetic: 2.61 us -> none  [the longest x1 1.85 us: per_device(): jnp.sum(jnp.where((pair_owner[:, None] == peers[None, :])[:, :, None], se...]
    unnamed x15, local copies, waits for them, and re-layouts: 4.32 us -> 2.09 us
    pallas_call x1 -> x2, Pallas kernels: 8.65 us -> 6.75 us  [the longest x1 5.99 us: per_device(): pl.pallas_call(functools.partial(pack_kernel, slot_cap), out_shape=jax.Sh...]
    all_to_all x1, waiting for transfers between devices: 24 us -> 22.2 us  [per_device(): lax.all_to_all(replies.reshape(devices, slot_cap, back_width), 'ctx', spl...]
  transfers between devices with their start and end apart: 2 -> 2, of which waited for: 2 -> 2; matrix products, arithmetic and copies ran while one was open for 0% -> 1% of each run, Pallas kernels for 13% -> 15%
where the time goes in v2:
time: 142 us
  waiting for transfers between devices  81.5 us (57%)
  Pallas kernels  37.3 us (26%)
  starting transfers between devices  19.3 us (14%)
  local copies, waits for them, and re-layouts  2.22 us (2%)
    all_to_all x1, waiting for transfers between devices, per_device(): lax.all_to_all(outgoing.reshape(devices, slot_cap, sent_width), 'ctx', sp...  59.3 us
    all_to_all x1, waiting for transfers between devices, per_device(): lax.all_to_all(replies.reshape(devices, slot_cap, back_width), 'ctx', spl...  22.2 us
    pallas_call x1, Pallas kernels, per_device(): pl.pallas_call(functools.partial(local_kernel, heads, size), out_shape=(w...  20.8 us
    all_to_all x1, starting transfers between devices, per_device(): lax.all_to_all(outgoing.reshape(devices, slot_cap, sent_width), 'ctx', sp...  13 us
    all_to_all x1, starting transfers between devices, per_device(): lax.all_to_all(replies.reshape(devices, slot_cap, back_width), 'ctx', spl...  6.28 us
    pallas_call x1, Pallas kernels, per_device(): pl.pallas_call(functools.partial(pack_kernel, slot_cap), out_shape=jax.Sh...  5.99 us
    pallas_call x1, Pallas kernels, per_device(): pl.pallas_call(functools.partial(combine_kernel, half), out_shape=(whole,...  5.72 us
    pallas_call x1, Pallas kernels, per_device(): pl.pallas_call(functools.partial(cross_kernel, kept, size, half), out_sha...  4.03 us
  transfers between devices with their start and end apart: 2, of which 2 were waited for; matrix products, arithmetic and copies ran while one was open for 1% of the time, Pallas kernels for 15%

profile of v2, /device:TPU:1, one launch (start us, length us, event | category | flops | bytes accessed | tf_op | source)
XLA Modules:
  0.0 141.8 jit_solution(11046408209888329855)
XLA Ops:
  0.6 6.0 %shard_map.122 = bf16[512,2432]{1,0:T(8,128)(2,1)} custom-call(s32[1,64]{1,0:T(1,128)} %bitcast.17, s32[8,64]{1,0:T(8,128)} %bitcast.15, bf16[16,640]{1,0:T(8,128)(2,1)} %bitcast.21, bf16[16,640]{1,0:T(8,128)(2,1)} %bitcast.23, bf16[640,1152]{1,0:T(8,128)(2,1)} %q_ref.1, bf16[640,1152]{1,0:T(8,128)(2,1)} %v_ref.1, bf16[640,1152]{1,0:T(8,128)(2,1)} %k_ref.1, ...), custom_call_target="tpu_custom_call" | custom-call | tf_op jit(solution)/shard_map/pallas_call | solution.py:281
  6.6 0.0 copy-start.6
  6.6 13.0 %all-to-all-start = ((bf16[64,8,2432]{2,1,0:T(8,128)(2,1)}), bf16[64,8,2432]{2,1,0:T(8,128)(2,1)S(1)}, u32[]{:S(2)}, u32[]{:S(2)}) async-start(bf16[64,8,2432]{2,1,0:T(8,128)(2,1)} %bitcast.19), calls=%async_computation | async-start | bytes 4980736 | tf_op jit(solution)/shard_map/all_to_all | solution.py:303
  19.7 0.0 copy-done.6
  19.7 0.1 copy.17.slots_ref
  19.8 59.3 %all-to-all-done = bf16[64,8,2432]{2,1,0:T(8,128)(2,1)S(1)} async-done(((bf16[64,8,2432]{2,1,0:T(8,128)(2,1)}), bf16[64,8,2432]{2,1,0:T(8,128)(2,1)S(1)}, u32[]{:S(2)}, u32[]{:S(2)}) %all-to-all-start) | async-done | bytes 2490400 | tf_op jit(solution)/shard_map/all_to_all | solution.py:303
  79.1 4.0 %shard_map.123 = bf16[512,1792]{1,0:T(8,128)(2,1)S(1)} custom-call(s32[256,1]{1,0:T(8,128)S(1)} %copy.17.slots_ref, bf16[512,2432]{1,0:T(8,128)(2,1)S(1)} %bitcast.12), custom_call_target="tpu_custom_call" | custom-call | tf_op jit(solution)/shard_map/pallas_call | solution.py:319
  83.1 0.0 copy-start
  83.2 1.2 copy-done
  84.4 0.0 copy-start.1
  84.4 0.0 copy-start.2
  84.4 0.0 copy-start.4
  84.4 6.3 %all-to-all-start.1 = ((bf16[64,8,1792]{2,1,0:T(8,128)(2,1)}), bf16[64,8,1792]{2,1,0:T(8,128)(2,1)S(1)}, u32[]{:S(2)}, u32[]{:S(2)}) async-start(bf16[64,8,1792]{2,1,0:T(8,128)(2,1)} %bitcast.14), calls=%async_computation.1 | async-start | bytes 3670016 | tf_op jit(solution)/shard_map/all_to_all | solution.py:329
  90.7 0.0 copy-done.1
  90.7 0.0 copy-done.2
  90.7 0.8 shard_map.121.codes_ref
  91.5 0.0 copy-done.5
  91.5 0.8 copy.18
  92.3 0.0 copy-done.3
  92.3 0.0 copy-done.4
  92.3 0.6 pad_maximum_fusion.stats_ref
  92.9 20.8 %shard_map.124 = (bf16[640,1152]{1,0:T(8,128)(2,1)}, bf16[640,1152]{1,0:T(8,128)(2,1)}, bf16[640,1152]{1,0:T(8,128)(2,1)}) custom-call(s32[256,2]{1,0:T(8,128)} %bitcast.20, bf16[640,1152]{1,0:T(8,128)(2,1)} %q_ref.1, bf16[640,1152]{1,0:T(8,128)(2,1)} %k_ref.1, bf16[640,1152]{1,0:T(8,128)(2,1)} %v_ref.1, bf16[640,1152]{1,0:T(8,128)(2,1)} %g_ref.1, ...), custom_call_target="tpu_custom_call" | custom-call | tf_op jit(solution)/shard_map/pallas_call | solution.py:309
  113.8 22.2 %all-to-all-done.1 = bf16[64,8,1792]{2,1,0:T(8,128)(2,1)S(1)} async-done(((bf16[64,8,1792]{2,1,0:T(8,128)(2,1)}), bf16[64,8,1792]{2,1,0:T(8,128)(2,1)S(1)}, u32[]{:S(2)}, u32[]{:S(2)}) %all-to-all-start.1) | async-done | bytes 1835040 | tf_op jit(solution)/shard_map/all_to_all | solution.py:329
  135.9 5.7 %shard_map.125 = (bf16[640,1152]{1,0:T(8,128)(2,1)}, bf16[640,1152]{1,0:T(8,128)(2,1)}, bf16[640,1152]{1,0:T(8,128)(2,1)}) custom-call(s32[8,512]{1,0:T(8,128)S(1)} %shard_map.121.codes_ref, bf16[512,1792]{1,0:T(8,128)(2,1)S(1)} %bitcast.13, bf16[640,1152]{1,0:T(8,128)(2,1)} %get-tuple-element.9.lq_hbm, ...), custom_call_target="tpu_custom_call", output_to_operand_aliasing={{0}: (2, {}), {1}: (3, {}), {2}: (4, {})} | custom-call | tf_op jit(solution)/shard_map/pallas_call | solution.py:339
  (2 shorter events, 0.0 us)
Async XLA Ops:
  6.6 13.0 %copy-start.6 = (s32[1,256]{1,0:T(1,128)S(1)}, s32[1,256]{1,0:T(1,128)}, u32[]{:S(2)}) copy-start(s32[1,256]{1,0:T(1,128)} %param.18) | copy-start | bytes 3076
  6.6 72.5 %all-to-all-start = ((bf16[64,8,2432]{2,1,0:T(8,128)(2,1)}), bf16[64,8,2432]{2,1,0:T(8,128)(2,1)S(1)}, u32[]{:S(2)}, u32[]{:S(2)}) async-start(bf16[64,8,2432]{2,1,0:T(8,128)(2,1)} %bitcast.19), calls=%async_computation | async-start | bytes 4980736 | tf_op jit(solution)/shard_map/all_to_all | solution.py:303
  83.1 1.3 copy-start
  84.4 6.3 %copy-start.1 = (s32[1,64,8]{1,2,0:T(8,128)S(1)}, s32[1,64,8]{1,2,0:T(8,128)}, u32[]{:S(2)}) copy-start(s32[1,64,8]{1,2,0:T(8,128)} %param.17) | copy-start | bytes 6148
  84.4 6.3 %copy-start.2 = (s32[64]{0:T(128)S(1)}, s32[64]{0:T(128)}, u32[]{:S(2)}) copy-start(s32[64]{0:T(128)} %param.19) | copy-start | bytes 772
  84.4 7.1 %copy-start.5 = (s32[2,256]{1,0:T(2,128)S(1)}, s32[2,256]{1,0:T(2,128)}, u32[]{:S(2)}) copy-start(s32[2,256]{1,0:T(2,128)} %param.16) | copy-start | bytes 6148
  84.4 7.9 %copy-start.3 = (bf16[640,16]{0,1:T(8,128)(2,1)S(1)}, bf16[640,16]{0,1:T(8,128)(2,1)}, u32[]{:S(2)}) copy-start(bf16[640,16]{0,1:T(8,128)(2,1)} %param.14) | copy-start | bytes 61444
  84.4 7.9 %copy-start.4 = (bf16[640,16]{0,1:T(8,128)(2,1)S(1)}, bf16[640,16]{0,1:T(8,128)(2,1)}, u32[]{:S(2)}) copy-start(bf16[640,16]{0,1:T(8,128)(2,1)} %param.15) | copy-start | bytes 61444
  84.4 51.5 %all-to-all-start.1 = ((bf16[64,8,1792]{2,1,0:T(8,128)(2,1)}), bf16[64,8,1792]{2,1,0:T(8,128)(2,1)S(1)}, u32[]{:S(2)}, u32[]{:S(2)}) async-start(bf16[64,8,1792]{2,1,0:T(8,128)(2,1)} %bitcast.14), calls=%async_computation.1 | async-start | bytes 3670016 | tf_op jit(solution)/shard_map/all_to_all | solution.py:329

commit v3 on v2

--- a/solution.py
+++ b/solution.py
@@ -155,7 +155,8 @@
         starts[order[0, at]] = (at & 1) * pair_rows + at // 2 * slot_cap
 
     kept = lse.shape[0] // 2
-    spans = (0, width, 2 * width, sent_width)
+    edge = half // LANES * LANES
+    spans = (0, edge, width, width + edge, 2 * width, sent_width)
     stores = [
         pltpu.make_async_copy(out.at[:, low:high], out_hbm.at[:, low:high], out_sems.at[at])
         for at, (low, high) in enumerate(zip(spans, spans[1:]))
@@ -171,30 +172,36 @@
             out[device * slot_cap : (device + 2) * slot_cap, span] = jnp.concatenate(both, 0).astype(jnp.bfloat16)
         stores[at].start()
 
+    def multiply(at, pieces):
+        for part in range(2):
+            ranked[part * pair_rows : (part + 1) * pair_rows, spans[at] : spans[at + 1]] = dot(pick, pieces(part))
+        deliver(at)
+
     for at in range(2):
+        one, two = sources[2 * at], sources[2 * at + 1]
         loads[3 + 4 * at].wait()
+        multiply(2 * at, lambda part: one[:, part * half : part * half + edge])
         loads[4 + 4 * at].wait()
-        one, two = sources[2 * at], sources[2 * at + 1]
-        for part in range(2):
-            cut = slice(part * half, (part + 1) * half)
-            ranked[part * pair_rows : (part + 1) * pair_rows, spans[at] : spans[at + 1]] = dot(
-                pick, jnp.concatenate([one[:, cut], two[:, cut]], 1)
-            )
-        deliver(at)
+        multiply(
+            2 * at + 1,
+            lambda part: jnp.concatenate(
+                [one[:, part * half + edge : (part + 1) * half], two[:, part * half : (part + 1) * half]], 1
+            ),
+        )
         if at == 0:
             loads[5].wait()
             loads[6].wait()
             for part in range(2):
                 cut = slice(part * kept, (part + 1) * kept)
                 stats = dot(pick, jnp.concatenate([lse[cut], delta[cut]], 0), NT)
-                fill = jnp.zeros((pair_rows, sent_width - spans[2] - 2 * kept), jnp.float32)
-                ranked[part * pair_rows : (part + 1) * pair_rows, spans[2] :] = jnp.concatenate([stats, fill], 1)
-            deliver(2)
+                fill = jnp.zeros((pair_rows, sent_width - spans[4] - 2 * kept), jnp.float32)
+                ranked[part * pair_rows : (part + 1) * pair_rows, spans[4] :] = jnp.concatenate([stats, fill], 1)
+            deliver(4)
     for store in stores:
         store.wait()
 
 
-def cross_kernel(heads, size, half, slots_ref, arrived_ref, out_ref, rows, sums, stat_rows):
+def cross_kernel(heads, size, half, slots_ref, arrived_ref, out_hbm, rows, sums, stat_rows, out, sems):
     win, count = slots_ref.shape[0], arrived_ref.shape[0]
     picker = (slots_ref[...] == lax.broadcasted_iota(jnp.int32, (win, count), 1)).astype(jnp.bfloat16)
     picked = dot(picker, arrived_ref[...])
@@ -214,7 +221,13 @@
         (sums, 2 * half),
         (sums, half),
     )
-    out_ref[...] = dot(picker, sums[...].astype(jnp.bfloat16), TN).astype(jnp.bfloat16)
+    stores = []
+    for at, cut in enumerate((slice(0, 2 * half), slice(2 * half, out.shape[1]))):
+        out[:, cut] = dot(picker, sums[:, cut].astype(jnp.bfloat16), TN).astype(jnp.bfloat16)
+        stores.append(pltpu.make_async_copy(out.at[:, cut], out_hbm.at[:, cut], sems.at[at]))
+        stores[at].start()
+    for store in stores:
+        store.wait()
 
 
 def combine_kernel(
@@ -296,7 +309,7 @@
             pltpu.VMEM((slots, sent_width), f32),
             pltpu.VMEM((slots, sent_width), bf16),
             pltpu.SemaphoreType.DMA((9,)),
-            pltpu.SemaphoreType.DMA((3,)),
+            pltpu.SemaphoreType.DMA((5,)),
         ],
         compiler_params=vmem(62),
     )(owner_line, send_lines, lse_lines, delta_lines, query_rows, value_rows, key_rows, out_grad)
@@ -318,12 +331,15 @@
     back_width = up(3 * half)
     replies = pl.pallas_call(
         functools.partial(cross_kernel, kept, size, half),
-        out_shape=jax.ShapeDtypeStruct((slots, back_width), bf16),
+        out_shape=pltpu.HBM((slots, back_width), bf16),
         scratch_shapes=[
             pltpu.VMEM((win, sent_width), bf16),
             pltpu.VMEM((win, back_width), f32),
             pltpu.VMEM((sent_width - 4 * half, win), f32),
+            pltpu.VMEM((slots, back_width), bf16),
+            pltpu.SemaphoreType.DMA((2,)),
         ],
+        out_specs=far,
         compiler_params=vmem(32),
     )(window_slots.reshape(win, 1), arrived)
     returned = lax.all_to_all(

time: 142 us -> 142 us (level)
  no operation moved by 1% of the time
where the time goes in v3:
time: 142 us
  waiting for transfers between devices  81.5 us (57%)
  Pallas kernels  38.3 us (27%)
  starting transfers between devices  19.3 us (14%)
    all_to_all x1, waiting for transfers between devices, per_device(): lax.all_to_all(outgoing.reshape(devices, slot_cap, sent_width), 'ctx', sp...  59.3 us
    all_to_all x1, waiting for transfers between devices, per_device(): lax.all_to_all(replies.reshape(devices, slot_cap, back_width), 'ctx', spl...  22.2 us
    pallas_call x1, Pallas kernels, per_device(): pl.pallas_call(functools.partial(local_kernel, heads, size), out_shape=(w...  20.8 us
    all_to_all x1, starting transfers between devices, per_device(): lax.all_to_all(outgoing.reshape(devices, slot_cap, sent_width), 'ctx', sp...  13 us
    all_to_all x1, starting transfers between devices, per_device(): lax.all_to_all(replies.reshape(devices, slot_cap, back_width), 'ctx', spl...  6.28 us
    pallas_call x1, Pallas kernels, per_device(): pl.pallas_call(functools.partial(pack_kernel, slot_cap), out_shape=jax.Sh...  5.89 us
    pallas_call x1, Pallas kernels, per_device(): pl.pallas_call(functools.partial(combine_kernel, half), out_shape=(whole,...  5.72 us
    pallas_call x1, Pallas kernels, per_device(): pl.pallas_call(functools.partial(cross_kernel, kept, size, half), out_sha...  5.09 us
  transfers between devices with their start and end apart: 2, of which 2 were waited for; matrix products, arithmetic and copies ran while one was open for 1% of the time, Pallas kernels for 15%

profile of v3, /device:TPU:1, one launch (start us, length us, event | category | flops | bytes accessed | tf_op | source)
XLA Modules:
  0.0 141.6 jit_solution(4915325746879930055)
XLA Ops:
  0.6 5.9 %shard_map.122 = bf16[512,2432]{1,0:T(8,128)(2,1)} custom-call(s32[1,64]{1,0:T(1,128)} %bitcast.16, s32[8,64]{1,0:T(8,128)} %bitcast.14, bf16[16,640]{1,0:T(8,128)(2,1)} %bitcast.21, bf16[16,640]{1,0:T(8,128)(2,1)} %bitcast.23, bf16[640,1152]{1,0:T(8,128)(2,1)} %q_ref.1, bf16[640,1152]{1,0:T(8,128)(2,1)} %v_ref.1, bf16[640,1152]{1,0:T(8,128)(2,1)} %k_ref.1, ...), custom_call_target="tpu_custom_call" | custom-call | tf_op jit(solution)/shard_map/pallas_call | solution.py:294
  6.5 0.0 copy-start.5
  6.5 13.0 %all-to-all-start = ((bf16[64,8,2432]{2,1,0:T(8,128)(2,1)}), bf16[64,8,2432]{2,1,0:T(8,128)(2,1)S(1)}, u32[]{:S(2)}, u32[]{:S(2)}) async-start(bf16[64,8,2432]{2,1,0:T(8,128)(2,1)} %bitcast.18), calls=%async_computation | async-start | bytes 4980736 | tf_op jit(solution)/shard_map/all_to_all | solution.py:316
  19.6 0.0 copy-done.5
  19.6 0.1 copy.17.slots_ref
  19.7 59.3 %all-to-all-done = bf16[64,8,2432]{2,1,0:T(8,128)(2,1)S(1)} async-done(((bf16[64,8,2432]{2,1,0:T(8,128)(2,1)}), bf16[64,8,2432]{2,1,0:T(8,128)(2,1)S(1)}, u32[]{:S(2)}, u32[]{:S(2)}) %all-to-all-start) | async-done | bytes 2490400 | tf_op jit(solution)/shard_map/all_to_all | solution.py:316
  79.0 5.1 %shard_map.123 = bf16[512,1792]{1,0:T(8,128)(2,1)} custom-call(s32[256,1]{1,0:T(8,128)S(1)} %copy.17.slots_ref, bf16[512,2432]{1,0:T(8,128)(2,1)S(1)} %bitcast.12), custom_call_target="tpu_custom_call" | custom-call | tf_op jit(solution)/shard_map/pallas_call | solution.py:332
  84.1 0.0 copy-start
  84.1 0.0 copy-start.1
  84.1 0.0 copy-start.4
  84.1 0.0 copy-start.2
  84.2 0.0 copy-start.3
  84.2 6.3 %all-to-all-start.1 = ((bf16[64,8,1792]{2,1,0:T(8,128)(2,1)}), bf16[64,8,1792]{2,1,0:T(8,128)(2,1)S(1)}, u32[]{:S(2)}, u32[]{:S(2)}) async-start(bf16[64,8,1792]{2,1,0:T(8,128)(2,1)} %bitcast.19), calls=%async_computation.1 | async-start | bytes 3670016 | tf_op jit(solution)/shard_map/all_to_all | solution.py:345
  90.5 0.0 copy-done
  90.5 0.0 copy-done.1
  90.5 0.8 shard_map.121.codes_ref
  91.2 0.0 copy-done.4
  91.2 0.8 copy.18
  92.0 0.0 copy-done.2
  92.0 0.0 copy-done.3
  92.1 0.6 pad_maximum_fusion.stats_ref
  92.7 20.8 %shard_map.124 = (bf16[640,1152]{1,0:T(8,128)(2,1)}, bf16[640,1152]{1,0:T(8,128)(2,1)}, bf16[640,1152]{1,0:T(8,128)(2,1)}) custom-call(s32[256,2]{1,0:T(8,128)} %bitcast.20, bf16[640,1152]{1,0:T(8,128)(2,1)} %q_ref.1, bf16[640,1152]{1,0:T(8,128)(2,1)} %k_ref.1, bf16[640,1152]{1,0:T(8,128)(2,1)} %v_ref.1, bf16[640,1152]{1,0:T(8,128)(2,1)} %g_ref.1, ...), custom_call_target="tpu_custom_call" | custom-call | tf_op jit(solution)/shard_map/pallas_call | solution.py:322
  113.5 22.2 %all-to-all-done.1 = bf16[64,8,1792]{2,1,0:T(8,128)(2,1)S(1)} async-done(((bf16[64,8,1792]{2,1,0:T(8,128)(2,1)}), bf16[64,8,1792]{2,1,0:T(8,128)(2,1)S(1)}, u32[]{:S(2)}, u32[]{:S(2)}) %all-to-all-start.1) | async-done | bytes 1835040 | tf_op jit(solution)/shard_map/all_to_all | solution.py:345
  135.7 5.7 %shard_map.125 = (bf16[640,1152]{1,0:T(8,128)(2,1)}, bf16[640,1152]{1,0:T(8,128)(2,1)}, bf16[640,1152]{1,0:T(8,128)(2,1)}) custom-call(s32[8,512]{1,0:T(8,128)S(1)} %shard_map.121.codes_ref, bf16[512,1792]{1,0:T(8,128)(2,1)S(1)} %bitcast.13, bf16[640,1152]{1,0:T(8,128)(2,1)} %get-tuple-element.9.lq_hbm, ...), custom_call_target="tpu_custom_call", output_to_operand_aliasing={{0}: (2, {}), {1}: (3, {}), {2}: (4, {})} | custom-call | tf_op jit(solution)/shard_map/pallas_call | solution.py:355
Async XLA Ops:
  6.5 13.0 %copy-start.5 = (s32[1,256]{1,0:T(1,128)S(1)}, s32[1,256]{1,0:T(1,128)}, u32[]{:S(2)}) copy-start(s32[1,256]{1,0:T(1,128)} %param.18) | copy-start | bytes 3076
  6.5 72.5 %all-to-all-start = ((bf16[64,8,2432]{2,1,0:T(8,128)(2,1)}), bf16[64,8,2432]{2,1,0:T(8,128)(2,1)S(1)}, u32[]{:S(2)}, u32[]{:S(2)}) async-start(bf16[64,8,2432]{2,1,0:T(8,128)(2,1)} %bitcast.18), calls=%async_computation | async-start | bytes 4980736 | tf_op jit(solution)/shard_map/all_to_all | solution.py:316
  84.1 6.4 %copy-start = (s32[1,64,8]{1,2,0:T(8,128)S(1)}, s32[1,64,8]{1,2,0:T(8,128)}, u32[]{:S(2)}) copy-start(s32[1,64,8]{1,2,0:T(8,128)} %param.17) | copy-start | bytes 6148
  84.1 6.3 %copy-start.1 = (s32[64]{0:T(128)S(1)}, s32[64]{0:T(128)}, u32[]{:S(2)}) copy-start(s32[64]{0:T(128)} %param.19) | copy-start | bytes 772
  84.1 7.1 %copy-start.4 = (s32[2,256]{1,0:T(2,128)S(1)}, s32[2,256]{1,0:T(2,128)}, u32[]{:S(2)}) copy-start(s32[2,256]{1,0:T(2,128)} %param.16) | copy-start | bytes 6148
  84.1 7.9 %copy-start.2 = (bf16[640,16]{0,1:T(8,128)(2,1)S(1)}, bf16[640,16]{0,1:T(8,128)(2,1)}, u32[]{:S(2)}) copy-start(bf16[640,16]{0,1:T(8,128)(2,1)} %param.14) | copy-start | bytes 61444
  84.2 7.9 %copy-start.3 = (bf16[640,16]{0,1:T(8,128)(2,1)S(1)}, bf16[640,16]{0,1:T(8,128)(2,1)}, u32[]{:S(2)}) copy-start(bf16[640,16]{0,1:T(8,128)(2,1)} %param.15) | copy-start | bytes 61444
  84.2 51.5 %all-to-all-start.1 = ((bf16[64,8,1792]{2,1,0:T(8,128)(2,1)}), bf16[64,8,1792]{2,1,0:T(8,128)(2,1)S(1)}, u32[]{:S(2)}, u32[]{:S(2)}) async-start(bf16[64,8,1792]{2,1,0:T(8,128)(2,1)} %bitcast.19), calls=%async_computation.1 | async-start | bytes 3670016 | tf_op jit(solution)/shard_map/all_to_all | solution.py:345
